TPU v7x, 128 devices: a whole 4x4x4 slice. The times are simulated.
128 devices in a mesh: pb: 64 (over z, x, y_lo, core), row: 2 (over y_hi).
Axes of the slice: x: 4, y: 4 (y_hi: 2, y_lo: 2; y = y_hi * 2 + y_lo), z: 4, core: 2. Of those that a mesh axis runs over, the one named last changes fastest.
Arguments:
- queries: bfloat16 [16384, 512], P('pb'), may hold values from -6 to 6
- references: bfloat16 [2, 4096, 512], P('row', 'pb'), may hold values from -6 to 6
- ratios: int32 [4, 2], replicated, may hold values from 1 to 3, as said below
- lengths: int32 [4], replicated, may hold values from 2 to 24, as said below
Outputs:
- enhanced: bfloat16 [16384, 8192], P('pb', 'row')
Inputs may be any that keep to these rules, and one draw needn't show every extreme that they name: `ratios`: the two steps of a direction differ, and no two directions have the same pair of steps. `lengths`: at least one direction has exactly 24 taps.
All inputs are finite; a program needn't handle non-finite values.
Results may differ from a plain program's by a relative error of at most 0.001.
Values may be sent and summed in bfloat16 or wider, within the bound.
A program may use at most 64 MiB of HBM per device.

v0:
```python
import math

import jax
import jax.numpy as jnp
from jax import lax
from jax.sharding import PartitionSpec as P

E = 512
NDIR = 4
LMAX = 24


def shifted_2(block, axis, distance):
    devices = range(lax.axis_size(axis))
    route = [(i - distance, i) for i in devices if i - distance in devices]
    return lax.ppermute(block, axis, route)


def offsets(ratios, lengths):
    tap_range = jnp.arange(LMAX, dtype=jnp.int32)
    steps_query = ratios[:, 0]
    steps_ref = ratios[:, 1]
    larger = jnp.maximum(steps_query, steps_ref)
    along_query = tap_range[None, :] * steps_query[:, None] // larger[:, None]
    along_ref = tap_range[None, :] * steps_ref[:, None] // larger[:, None]
    inverse = 1.0 / lengths.astype(jnp.float32)
    tap_weights = jnp.where(tap_range[None, :] < lengths[:, None], inverse[:, None], 0.0)
    return (along_query, along_ref, tap_weights)


def smooth(similarity, along_query, along_ref, tap_weights, row_count, col_count):
    strongest = None
    for direction in range(NDIR):
        running = jnp.zeros((row_count, col_count), jnp.float32)
        for tap_index in range(LMAX):
            shifted = lax.dynamic_slice(
                similarity,
                (along_query[direction, tap_index], along_ref[direction, tap_index]),
                (row_count, col_count),
            )
            running = running + tap_weights[direction, tap_index] * shifted
        strongest = running if strongest is None else jnp.maximum(strongest, running)
    return strongest


def per_device(queries, references, ratios, lengths):
    along_query, along_ref, tap_weights = offsets(ratios, lengths)
    margin = LMAX - 1
    inv_root = 1.0 / math.sqrt(E)
    query_count = queries.shape[0]
    half_count = references.shape[1] * lax.axis_size("pb")
    block_rows = min(512, query_count)
    next_queries = shifted_2(queries[:margin], "pb", -1)
    extended_queries = jnp.concatenate([queries, next_queries], axis=0)
    gathered = lax.all_gather(references, "pb", axis=1, tiled=True)[0]
    ref_margin = shifted_2(gathered[:margin], "row", -1)
    extended_ref = jnp.concatenate([gathered, ref_margin], axis=0)

    def one_block(block_index):
        similarity = (
            jnp.einsum(
                "qe,re->qr", extended_queries, extended_ref, preferred_element_type=jnp.float32
            )
            * inv_root
        )
        return smooth(
            similarity, along_query, along_ref, tap_weights, block_rows, half_count
        ).astype(jnp.bfloat16)

    result = lax.map(one_block, jnp.arange(query_count // block_rows, dtype=jnp.int32))
    return result.reshape(query_count, half_count)


def solution(mesh):
    placed = (P("pb", None), P("row", "pb", None), P(), P())
    return jax.shard_map(
        per_device, mesh=mesh, in_specs=placed, out_specs=P("pb", "row"), check_vma=False
    )
```

profile of v0, /device:TPU:1, one launch (start us, length us, event | category | flops | bytes accessed | tf_op | source)
XLA Modules:
  0.0 812.7 jit_solution(1302173895661448995)
XLA Ops:
  6.5 0.0 all-gather.2.cloned.1.call-start
  6.5 0.7 all-gather.2.cloned.1.call-update
  7.3 0.7 slice.1168
  8.0 3.3 collective-permute-start
  11.3 0.8 slice_bitcast_fusion.1
  12.1 0.2 add_select_fusion
  12.3 0.7 slice.1186
  14.3 0.7 fusion.16
  39.0 0.7 fusion.24
  63.4 0.7 fusion.22
  87.9 0.7 fusion.20
  112.5 0.7 fusion.18
  136.8 0.6 slice.1185
  138.7 0.7 fusion.17
  162.7 0.7 fusion.25
  168.8 0.7 convert_divide_fusion
  169.4 0.7 fusion.8
  170.2 0.6 slice.1167
  170.7 0.7 fusion.23
  171.5 0.7 fusion.21
  172.2 0.7 fusion.14
  172.9 0.7 fusion.13
  173.7 0.7 fusion.15
  174.4 0.7 fusion.19
  175.1 0.7 fusion.12
  175.9 0.7 fusion.11
  176.6 0.0 all-gather.2.cloned.1.call-done
  176.6 0.7 slice_bitcast_fusion
  177.4 1.3 collective-permute-start.1
  388.9 0.0 collective-permute-done
  388.9 0.0 collective-permute-done.1
  388.9 3.7 convolution_multiply_fusion
  392.7 0.0 copy-start
  392.7 3.8 dynamic-slice_multiply_fusion
  396.5 0.0 copy-done
  396.5 409.3 %maximum_convert_fusion = bf16[256,4096]{1,0:T(8,128)(2,1)} fusion(f32[279,4119]{1,0:T(8,128)} %copy-done, s32[]{:T(128)S(6)} %select_n.967, s32[]{:T(128)S(6)} %select_n.968, s32[]{:T(128)S(6)} %select_n.965, s32[]{:T(128)S(6)} %select_n.966, s32[]{:T(128)S(6)} %select_n.963, s32[]{:T(128)S(6)} %select_n.964, s32[]{:T(128)S(6)} %select_n.961, ...), kind=kLoop, calls=%fused_computation.4 | loop fusion | flops 200278016 | bytes 404751488 | tf_op jit(solution)/shard_map/while/body/eval_jaxpr/convert_element_type | solution.py:68
Async XLA Ops:
  6.5 170.1 %all-gather.2.cloned.1.call-start = ((), (), s32[]{:S(2)}) async-start(), calls=%async_computation | async-start | bytes 4259840 | tf_op jit(solution)/shard_map/all_gather | solution.py:55
  8.0 380.9 %collective-permute-start = (bf16[23,512]{1,0:T(8,128)(2,1)S(1)}, bf16[23,512]{1,0:T(8,128)(2,1)S(1)}, u32[]{:S(2)}, u32[]{:S(2)}) collective-permute-start(bf16[23,512]{1,0:T(8,128)(2,1)S(1)} %slice.1168), channel_id=1, source_target_pairs={{2,0},{4,2},{6,4},{8,6},{10,8},{12,10},{14,12},{16,14},{18,16},{20... | collective-permute-start | bytes 70664 | tf_op jit(solution)/shard_map/ppermute | solution.py:16
  177.4 211.6 %collective-permute-start.1 = (bf16[23,512]{1,0:T(8,128)(2,1)S(1)}, bf16[23,512]{1,0:T(8,128)(2,1)S(1)}, u32[]{:S(2)}, u32[]{:S(2)}) collective-permute-start(bf16[23,512]{1,0:T(8,128)(2,1)S(1)} %slice_bitcast_fusion), channel_id=1, source_target_pairs={{1,0},{3,2},{5,4},{7,6},{9,8},{11,10},{13,12},{15,14},{17,16},{19,... | collective-permute-start | bytes 70664 | tf_op jit(solution)/shard_map/ppermute | solution.py:16
  392.7 3.8 copy-start
Sparse Core Ops, SparseCore 0:
  9.1 109.6 all-gather.1
where the time goes:
time: 823 us; the launch traced here: 813 us
  other arithmetic  415 us (50%)
  between operations  374 us (45%)
  local copies, waits for them, and re-layouts  14.3 us (2%)
    convert_element_type x1, other arithmetic, one_block(): return smooth(similarity, along_query, along_ref, tap_weights, block_rows...  409 us
  transfers between devices with their start and end apart: 3, of which 0 were waited for; matrix products, arithmetic and copies ran while one was open for 2% of the time, Pallas kernels for 0%

commit v1 on v0

v1 whole, which is shorter than its diff:
```python
import functools
import math

import jax
import jax.numpy as jnp
from jax import lax
from jax.experimental import pallas as pl
from jax.experimental.pallas import tpu as pltpu
from jax.sharding import PartitionSpec as P

E = 512
MESH = pl.DeviceIdType.MESH
TAIL = 32


def gather(q_ref, r_ref, g, qh, rh, local, ysem, u1, u2, v1, v2, sib, hsem):
    pb, row = lax.axis_index("pb"), lax.axis_index("row")
    pbs = 64
    c, y, x, z = pb & 1, (pb >> 1) & 1, (pb >> 2) & 3, pb >> 4

    def at(z_, x_, y_, c_):
        return ((z_ * 4 + x_) * 2 + y_) * 2 + c_

    me = (z, x)
    def place(axis, k):
        return (z, (x + k) & 3) if axis == 0 else ((z + k) & 3, x)

    left = [at(*place(a, 3), y, c) for a in range(2)]
    right = [at(*place(a, 1), y, c) for a in range(2)]
    other_y = at(z, x, 1 - y, c)
    other_c = at(z, x, y, 1 - c)

    bar = pltpu.get_barrier_semaphore()
    for dev in (left[0], right[0], left[1], right[1], other_y, other_c):
        pl.semaphore_signal(bar, inc=1, device_id={"pb": dev}, device_id_type=MESH)

    @pl.when(pb < pbs - 1)
    def _():
        pl.semaphore_signal(bar, inc=1, device_id={"pb": pb + 1}, device_id_type=MESH)

    @pl.when(row == 0)
    def _():
        pl.semaphore_signal(bar, inc=1, device_id={"row": 1}, device_id_type=MESH)
    pl.semaphore_wait(bar, 6 + jnp.minimum(pb, 1) + row)

    sends = []

    def send(src, dst, sems, k, dev):
        copy = pltpu.make_async_remote_copy(src_ref=src, dst_ref=dst, send_sem=sems.at[0, k], recv_sem=sems.at[1, k],
                                            device_id={"pb": dev}, device_id_type=MESH)
        copy.start()
        sends.append(copy)

    def arrived(dst, sems, k):
        pltpu.make_async_copy(dst, dst, sems.at[1, k]).wait()

    def block(zx, y_, c_, lo, size):
        return g.at[zx[0], zx[1], y_, c_, pl.ds(lo, size)]

    def pair(zx, c_, lo, size):
        return g.at[zx[0], zx[1], :, c_, pl.ds(lo, size)]

    own_block = block(me, y, c, 0, 64)
    keep = pltpu.make_async_copy(r_ref.at[0], own_block, local)
    keep.start()
    send(r_ref.at[0], own_block, ysem, 0, other_y)
    for h in range(2):
        mine = r_ref.at[0, pl.ds(32 * h, 32)]
        send(mine, block(me, y, c, 32 * h, 32), u1, h * 4 + 0, right[h])
        send(mine, block(me, y, c, 32 * h, 32), u1, h * 4 + 1, left[h])
    send(r_ref.at[0], own_block, sib, 0, other_c)
    first = pltpu.make_async_remote_copy(src_ref=q_ref.at[pl.ds(0, TAIL)], dst_ref=qh, send_sem=hsem.at[0, 0], recv_sem=hsem.at[1, 0],
                                         device_id={"pb": jnp.maximum(pb - 1, 0)}, device_id_type=MESH)

    @pl.when(pb > 0)
    def _():
        first.start()

    keep.wait()
    arrived(block(me, 1 - y, c, 0, 64), ysem, 0)
    for h in range(2):
        theirs = block(me, 1 - y, c, 32 * h, 32)
        send(theirs, theirs, u1, h * 4 + 2, right[h])
        send(theirs, theirs, u1, h * 4 + 3, left[h])
    far = [1, 0]
    for h in range(2):
        p = pair(me, c, 32 * h, 32)
        send(p, p, v1, h * 8 + 0, right[far[h]])
        send(p, p, v1, h * 8 + 1, left[far[h]])
    theirs = block(me, 1 - y, c, 0, 64)
    send(theirs, theirs, sib, 1, other_c)
    n = 2
    for h in range(2):
        for side, k in ((0, 3), (1, 1)):
            src = place(h, k)
            for w, y_ in ((0, y), (1, 1 - y)):
                arrived(block(src, y_, c, 32 * h, 32), u1, h * 4 + 2 * w + side)
                piece = block(src, y_, c, 32 * h + 16 * side, 16)
                send(piece, piece, u2, h * 4 + 2 * w + side, right[h] if side == 0 else left[h])
    for h in range(2):
        for side, k in ((0, 3), (1, 1)):
            p = pair(place(h, k), c, 32 * h, 32)
            send(p, p, v1, h * 8 + 2 + 2 * side, right[far[h]])
            send(p, p, v1, h * 8 + 3 + 2 * side, left[far[h]])
            send(p, p, sib, n, other_c)
            n += 1
    for h in range(2):
        src = place(h, 2)
        for side in range(2):
            for w, y_ in ((0, y), (1, 1 - y)):
                arrived(block(src, y_, c, 32 * h + 16 * side, 16), u2, h * 4 + 2 * w + side)
        p = pair(src, c, 32 * h, 32)
        send(p, p, v1, h * 8 + 6, right[far[h]])
        send(p, p, v1, h * 8 + 7, left[far[h]])
        send(p, p, sib, n, other_c)
        n += 1

    def spot(h, k1, k2):
        return ((z + k2) & 3, (x + k1) & 3) if h == 0 else ((z + k1) & 3, (x + k2) & 3)

    steps = (0, 3, 1, 2)
    for j, k1 in enumerate(steps):
        for h in range(2):
            for side, k2 in ((0, 3), (1, 1)):
                src = spot(h, k1, k2)
                p = pair(src, c, 32 * h, 32)
                arrived(p, v1, h * 8 + 2 * j + side)
                piece = pair(src, c, 32 * h + 16 * side, 16)
                send(piece, piece, v2, h * 8 + 2 * j + side, right[far[h]] if side == 0 else left[far[h]])
                send(p, p, sib, n, other_c)
                n += 1
    for j, k1 in enumerate(steps):
        for h in range(2):
            src = spot(h, k1, 2)
            for side in range(2):
                arrived(pair(src, c, 32 * h + 16 * side, 16), v2, h * 8 + 2 * j + side)
            p = pair(src, c, 32 * h, 32)
            send(p, p, sib, n, other_c)
            n += 1
    o = 1 - c
    arrived(block(me, y, o, 0, 64), sib, 0)
    arrived(block(me, 1 - y, o, 0, 64), sib, 1)
    n = 2
    for h in range(2):
        for k in (3, 1):
            arrived(pair(place(h, k), o, 32 * h, 32), sib, n)
            n += 1
    for h in range(2):
        arrived(pair(place(h, 2), o, 32 * h, 32), sib, n)
        n += 1
    for k1 in steps:
        for h in range(2):
            for k2 in (3, 1):
                arrived(pair(spot(h, k1, k2), o, 32 * h, 32), sib, n)
                n += 1
    for k1 in steps:
        for h in range(2):
            arrived(pair(spot(h, k1, 2), o, 32 * h, 32), sib, n)
            n += 1
    head = pltpu.make_async_remote_copy(src_ref=g.at[0, 0, 0, 0, pl.ds(0, TAIL)], dst_ref=rh, send_sem=hsem.at[0, 1], recv_sem=hsem.at[1, 1],
                                        device_id={"row": 0}, device_id_type=MESH)

    @pl.when(row == 1)
    def _():
        head.start()

    for copy in sends:
        copy.wait_send()

    @pl.when(pb > 0)
    def _():
        first.wait_send()

    @pl.when(pb < pbs - 1)
    def _():
        first.wait_recv()

    @pl.when(row == 1)
    def _():
        head.wait_send()

    @pl.when(row == 0)
    def _():
        head.wait_recv()


def call_gather(q, r):
    bf = jnp.bfloat16
    D = pltpu.SemaphoreType.DMA
    g, qh, rh = pl.pallas_call(
        gather,
        out_shape=(jax.ShapeDtypeStruct((4, 4, 2, 2, 64, E), bf), jax.ShapeDtypeStruct((TAIL, E), bf), jax.ShapeDtypeStruct((TAIL, E), bf)),
        in_specs=[pl.BlockSpec(memory_space=pl.ANY)] * 2,
        out_specs=[pl.BlockSpec(memory_space=pl.ANY)] * 3,
        scratch_shapes=[D, D((2, 1)), D((2, 8)), D((2, 8)), D((2, 16)), D((2, 16)), D((2, 32)), D((2, 2))],
        compiler_params=pltpu.CompilerParams(collective_id=0, has_side_effects=True),
        name="gather",
    )(q, r)
    return g.reshape(4096, E), qh, rh


NDIR = 4
LMAX = 24
B = 32
HALO = 24
PLANES = B + HALO
ZERO = 58
ROWS = 288
PAD = 296
SUPER = 32


def lane_iota(shape, d):
    return lax.broadcasted_iota(jnp.int32, shape, d)


def compute(ratios, lengths, q_ref, qh_ref, rh_ref, g_ref, out_ref,
            gv, qx, rb, s, d0, d1, d2, d3, e0, e1, e2, e3, o, perm, osb, gsem, osem):
    rows = q_ref.shape[0]
    cols = g_ref.shape[0]
    parts = 4
    part = cols // parts
    ds, es = (d0, d1, d2, d3), (e0, e1, e2, e3)
    copies = [pltpu.make_async_copy(g_ref.at[pl.ds(k * part, part)], gv.at[pl.ds(k * part, part)], gsem.at[k]) for k in range(parts)]
    for c in copies:
        c.start()
    qx[pl.ds(0, rows), :] = q_ref[...]
    keep_q = lax.axis_index("pb") < lax.axis_size("pb") - 1
    keep_r = lax.axis_index("row") == 0
    qx[pl.ds(rows, 32), :] = jnp.where(keep_q, qh_ref[...], jnp.zeros((32, E), jnp.bfloat16))
    rhv = jnp.where(keep_r, rh_ref[...], jnp.zeros((32, E), jnp.bfloat16))
    ps = [ratios[d, 0] for d in range(NDIR)]
    ss = [ratios[d, 1] for d in range(NDIR)]
    ms = [jnp.maximum(ps[d], ss[d]) for d in range(NDIR)]
    ns = [lax.div(lengths[d], ms[d]) for d in range(NDIR)]
    phase = [lengths[d] - ns[d] * ms[d] for d in range(NDIR)]
    weight = [1.0 / (lengths[d].astype(jnp.float32)) * (1.0 / math.sqrt(E)) for d in range(NDIR)]
    q1 = [lax.div(ps[d], ms[d]) for d in range(NDIR)]
    r1 = [lax.div(ss[d], ms[d]) for d in range(NDIR)]
    q2 = [lax.div(2 * ps[d], ms[d]) for d in range(NDIR)]
    r2 = [lax.div(2 * ss[d], ms[d]) for d in range(NDIR)]
    three = [ms[d] == 3 for d in range(NDIR)]
    zero = jnp.zeros((8, 128), jnp.float32)

    def clear(b, _):
        s[b, pl.ds(ROWS, 8), :] = zero
        return 0
    lax.fori_loop(0, ZERO, clear, 0)
    s[ZERO] = jnp.zeros((PAD, 128), jnp.float32)
    for b in range(PLANES, ZERO):
        s[b] = jnp.zeros((PAD, 128), jnp.float32)
    for d in range(NDIR):
        for k in range(4):
            ds[d][k] = jnp.zeros((PAD, 128), jnp.float32)

    la = lane_iota((128, 128), 0)
    ll = lane_iota((128, 128), 1)
    same = (la & 3) == (ll >> 5)
    def make(qi, _):
        hit = same & (((la >> 2) ^ (ll & 31)) == qi)
        perm[qi] = jnp.where(hit, 1.0, 0.0).astype(jnp.bfloat16)
        return 0
    lax.fori_loop(0, B, make, 0)

    ri = lane_iota((256, 256), 0)
    ci = lane_iota((256, 256), 1)
    turn = jnp.where(((ri >> 3) == (ci & 31)) & ((ri & 7) == (ci >> 5)), 1.0, 0.0).astype(jnp.bfloat16)
    for k in range(parts):
        copies[k].wait()
        def two(t, _):
            base = pl.multiple_of(k * part + t * 512, 512)
            x = jnp.dot(turn, gv[pl.ds(base, 256), :], preferred_element_type=jnp.float32).reshape(B, 8, E)
            y = jnp.dot(turn, gv[pl.ds(base + 256, 256), :], preferred_element_type=jnp.float32).reshape(B, 8, E)
            z = jnp.concatenate([x, y], axis=1).astype(jnp.bfloat16)
            rb[pl.ds(0, B), pl.ds(pl.multiple_of((k * part // 512 + t) * 16, 16), 16), :] = z
            return 0
        lax.fori_loop(0, part // 512, two, 0)
    def dots(t, _):
        w = rb[pl.ds(2 * t, 2)].reshape(256, E)
        v = lax.dot_general(qx[...], w, (((1,), (1,)), ((), ())), preferred_element_type=jnp.float32)
        s[2 * t, pl.ds(0, ROWS), :] = v[:, :128]
        s[2 * t + 1, pl.ds(0, ROWS), :] = v[:, 128:]
        return 0
    lax.fori_loop(0, B // 2, dots, 0)
    hi = lane_iota((128, 160), 0)
    hj = lane_iota((128, 160), 1)
    def halo(t, _):
        ws = []
        for u in range(2):
            x = 2 * t + u
            pick = jnp.where((hj == hi + 1) & (hi < 127) | (hi == 127) & (hj == 128 + x), 1.0, 0.0).astype(jnp.bfloat16)
            src = jnp.concatenate([rb[x], rhv], axis=0)
            ws.append(jnp.dot(pick, src, preferred_element_type=jnp.float32).astype(jnp.bfloat16))
        w = jnp.concatenate(ws, axis=0)
        v = lax.dot_general(qx[...], w, (((1,), (1,)), ((), ())), preferred_element_type=jnp.float32)
        s[B + 2 * t, pl.ds(0, ROWS), :] = v[:, :128]
        s[B + 2 * t + 1, pl.ds(0, ROWS), :] = v[:, 128:]
        return 0
    lax.fori_loop(0, HALO // 2, halo, 0)

    def step(d, b, row, count, s0):
        dp = ds[d][(b + ss[d]) & 3, pl.ds(row + ps[d], count), :]
        t2 = s[jnp.where(three[d], b + r2[d], ZERO), pl.ds(row + q2[d], count), :]
        t1 = s[b + r1[d], pl.ds(row + q1[d], count), :]
        x2 = dp + t2
        x1 = x2 + t1
        x0 = x1 + s0
        e = jnp.where(phase[d] == 0, x0, jnp.where(phase[d] == 1, x1, x2))
        return x0, e

    for d in range(NDIR):
        last = B - 1 + ns[d] * ss[d]
        def plane(k, _):
            b = last - k
            for r in range(0, ROWS, SUPER):
                s0 = s[b, pl.ds(r, SUPER), :]
                x0, e = step(d, b, r, SUPER, s0)
                ds[d][b & 3, pl.ds(r, SUPER), :] = x0
                es[d][b & 31, pl.ds(r, SUPER), :] = e
            return 0
        lax.fori_loop(0, last - (B - 1), plane, 0)

    def final(k, _):
        b = B - 1 - k
        for r in range(0, ROWS, SUPER):
            s0 = s[b, pl.ds(r, SUPER), :]
            best = None
            for d in range(NDIR):
                x0, e = step(d, b, r, SUPER, s0)
                ds[d][b & 3, pl.ds(r, SUPER), :] = x0
                es[d][b & 31, pl.ds(r, SUPER), :] = e
                if r < rows:
                    en = es[d][(b + ns[d] * ss[d]) & 31, pl.ds(r + ns[d] * ps[d], SUPER), :]
                    v = (x0 - en) * weight[d]
                    best = v if best is None else jnp.maximum(best, v)
            if r < rows:
                o[b, pl.ds(r, SUPER), :] = best.astype(jnp.bfloat16)
        return 0
    lax.fori_loop(0, B, final, 0)

    lane = lane_iota((16, 128), 1)
    def network(x, bits):
        for t in range(5):
            mask = ((lane >> (bits + t)) & 1) == 1
            x = [jnp.where(mask, x[q ^ (1 << t)], x[q]) for q in range(B)]
        return x
    def skew(i, _):
        r = pl.ds(pl.multiple_of(i * 16, 16), 16)
        x = network([o[q, r, :] for q in range(B)], 2)
        for q in range(B):
            o[q, r, :] = x[q]
        return 0
    lax.fori_loop(0, rows // 16, skew, 0)
    def turn_lanes(qi, _):
        o[qi] = jnp.dot(o[qi], perm[qi], preferred_element_type=jnp.float32).astype(jnp.bfloat16)
        return 0
    lax.fori_loop(0, B, turn_lanes, 0)
    def back(i, _):
        r = pl.ds(pl.multiple_of(i * 16, 16), 16)
        x = network([o[q, r, :] for q in range(B)], 0)
        for q in range(B):
            osb[r, q * 128:(q + 1) * 128] = x[q]
        return 0
    lax.fori_loop(0, rows // 16, back, 0)
    c = pltpu.make_async_copy(osb, out_ref, osem)
    c.start()
    c.wait()


def call_compute(ratios, lengths, q, qh, rh, g):
    rows, cols = q.shape[0], g.shape[0]
    f32, bf = jnp.float32, jnp.bfloat16
    V = pltpu.VMEM
    return pl.pallas_call(
        compute,
        out_shape=jax.ShapeDtypeStruct((rows, cols), bf),
        in_specs=[pl.BlockSpec(memory_space=pltpu.SMEM)] * 2 + [pl.BlockSpec(memory_space=V)] * 3 + [pl.BlockSpec(memory_space=pl.ANY)],
        out_specs=pl.BlockSpec(memory_space=pl.ANY),
        scratch_shapes=[V((cols, E), bf), V((ROWS, E), bf), V((B, 128, E), bf), V((ZERO + 1, PAD, 128), f32)]
        + [V((4, PAD, 128), f32)] * 4 + [V((32, PAD, 128), f32)] * 4
        + [V((B, rows, 128), bf), V((B, 128, 128), bf), V((rows, cols), bf), pltpu.SemaphoreType.DMA((4,)), pltpu.SemaphoreType.DMA],
        compiler_params=pltpu.CompilerParams(vmem_limit_bytes=60 * 1024 * 1024),
        name="smooth",
    )(ratios, lengths, q, qh, rh, g)


def per_device(queries, references, ratios, lengths):
    g, qh, rh = call_gather(queries, references)
    return call_compute(ratios, lengths, queries, qh, rh, g)


def solution(mesh):
    placed = (P("pb", None), P("row", "pb", None), P(), P())
    return jax.shard_map(
        per_device, mesh=mesh, in_specs=placed, out_specs=P("pb", "row"), check_vma=False
    )
```

time: 823 us -> 67.8 us (0.08); the launches traced: 813 us -> 67.6 us
  other arithmetic: 415 us -> 0 us
  between operations: 374 us -> 0.01 us
  Pallas kernels: 0 us -> 66.3 us
  local copies, waits for them, and re-layouts: 14.3 us -> 1.35 us
    convert_element_type x1 -> x0, other arithmetic: 409 us -> none  [one_block(): return smooth(similarity, along_query, along_ref, tap_weights, block_rows...]
    pallas_call x0 -> x2, Pallas kernels: none -> 66.3 us  [the longest x1 33.4 us: call_gather(): pl.pallas_call(gather, out_shape=(jax.ShapeDtypeStruct((4, 4, 2, 2, 64, E...]
    slice x20 -> x0, local copies, waits for them, and re-layouts: 14.3 us -> none  [the longest x6 4.35 us: smooth(): along_ref[direction, tap_index]]
  transfers between devices with their start and end apart: 3 -> 0, of which waited for: 0 -> 0; matrix products, arithmetic and copies ran while one was open for 2% -> 0% of each run, Pallas kernels for 0% -> 0%
where the time goes in v1:
time: 67.8 us; the launch traced here: 67.6 us
  Pallas kernels  66.3 us (98%)
  local copies, waits for them, and re-layouts  1.35 us (2%)
    pallas_call x1, Pallas kernels, call_gather(): pl.pallas_call(gather, out_shape=(jax.ShapeDtypeStruct((4, 4, 2, 2, 64, E...  33.4 us
    pallas_call x1, Pallas kernels, call_compute(): pl.pallas_call(compute, out_shape=jax.ShapeDtypeStruct((rows, cols), bf),...  32.9 us

profile of v1, /device:TPU:1, one launch (start us, length us, event | category | flops | bytes accessed | tf_op | source)
XLA Modules:
  0.0 67.6 jit_solution(9632940995196931604)
XLA Ops:
  0.0 1.4 %copy.5.ratios = s32[4,2]{1,0:T(4,128)} copy(s32[4,2]{0,1:T(2,128)} %param.6) | data formatting | bytes 64 | tf_op args[2]
  1.4 33.4 %gather.1 = (bf16[4,4,2,2,64,512]{5,4,3,2,1,0:T(8,128)(2,1)}, bf16[32,512]{1,0:T(8,128)(2,1)}, bf16[32,512]{1,0:T(8,128)(2,1)}) custom-call(bf16[256,512]{1,0:T(8,128)(2,1)} %q_ref.3, bf16[1,64,512]{2,1,0:T(8,128)(2,1)} %r_ref.1), custom_call_target="tpu_custom_call" | custom-call | tf_op jit(solution)/shard_map/gather/pallas_call | solution.py:190
  34.7 32.9 %smooth.1 = bf16[256,4096]{1,0:T(8,128)(2,1)} custom-call(s32[4,2]{1,0:T(4,128)} %copy.5.ratios, s32[4]{0:T(128)} %lengths.1, bf16[256,512]{1,0:T(8,128)(2,1)} %q_ref.3, bf16[32,512]{1,0:T(8,128)(2,1)} %get-tuple-element.8.qh_ref, bf16[32,512]{1,0:T(8,128)(2,1)} %get-tuple-element.9.rh_ref, bf16[4096,512]{1,0:T(8,128)(2,1)} %bitcast.1), custom_call_target="tpu_custom_call" | custom-call | tf_op jit(solution)/shard_map/smooth/pallas_call | solution.py:374

commit v2 on v0

v2 whole, which is shorter than its diff:
```python
import math

import jax
import jax.numpy as jnp
from jax import lax
from jax.experimental import pallas as pl
from jax.experimental.pallas import tpu as pltpu
from jax.sharding import PartitionSpec as P

E = 512
NDIR = 4
B = 32
HALO = 24
PLANES = B + HALO
ZERO = 58
TAIL = 32
PAD = 8
SUPER = 32
GROUP = 8
MESH = pl.DeviceIdType.MESH
F32, BF = jnp.float32, jnp.bfloat16


def iota(shape, d):
    return lax.broadcasted_iota(jnp.int32, shape, d)


def gather_and_smooth(steps_ref, lengths, q_ref, r_ref, o_ref,
                      gv, qx, rb, s, d0, d1, d2, d3, e0, e1, e2, e3, o,
                      local, ysem, u1, v1, far, v2, sib, qsem, hsem, osem):
    rows = q_ref.shape[0]
    all_rows = rows + TAIL
    ds, es = (d0, d1, d2, d3), (e0, e1, e2, e3)
    pb, row = lax.axis_index("pb"), lax.axis_index("row")
    c, y, x, z = pb & 1, (pb >> 1) & 1, (pb >> 2) & 3, pb >> 4
    last = pb == 63
    me = (z, x)

    def at(zx, y_, c_):
        return ((zx[0] * 4 + zx[1]) * 2 + y_) * 2 + c_

    def place(h, k):
        return (z, (x + k) & 3) if h == 0 else ((z + k) & 3, x)

    def spot(h, k1, k2):
        return ((z + k2) & 3, (x + k1) & 3) if h == 0 else ((z + k1) & 3, (x + k2) & 3)

    other_y, other_c = at(me, 1 - y, c), at(me, y, 1 - c)

    bar = pltpu.get_barrier_semaphore()
    peers = [other_y, other_c] + [at(place(h, k), y_, c) for h in range(2) for k in (1, 2, 3) for y_ in (0, 1)]
    for dev in peers:
        pl.semaphore_signal(bar, inc=1, device_id={"pb": dev}, device_id_type=MESH)

    @pl.when(pb < 63)
    def _():
        pl.semaphore_signal(bar, inc=1, device_id={"pb": pb + 1}, device_id_type=MESH)

    @pl.when(row == 0)
    def _():
        pl.semaphore_signal(bar, inc=1, device_id={"pb": at((0, x), y, 0), "row": 1}, device_id_type=MESH)

    heads = jnp.where((row == 1) & (z == 0) & (c == 0), 8, 0)
    pl.semaphore_wait(bar, len(peers) + jnp.minimum(pb, 1) + heads)

    sends = []

    def send(src, dst, sems, k, dev):
        copy = pltpu.make_async_remote_copy(src_ref=src, dst_ref=dst, send_sem=sems.at[0, k], recv_sem=sems.at[1, k],
                                            device_id={"pb": dev}, device_id_type=MESH)
        copy.start()
        sends.append(copy)

    def arrived(dst, sems, k):
        pltpu.make_async_copy(dst, dst, sems.at[1, k]).wait()

    def block(zx, y_, c_, lo, size):
        return gv.at[(zx[0] * 4 + zx[1]) * 2 + y_, pl.ds(c_ * 64 + lo, size)]

    def pair(zx, c_, lo, size):
        return gv.at[pl.ds((zx[0] * 4 + zx[1]) * 2, 2), pl.ds(c_ * 64 + lo, size)]

    own = r_ref.at[0]
    keep = pltpu.make_async_copy(own, block(me, y, c, 0, 64), local.at[0])
    keep.start()
    send(own, block(me, y, c, 0, 64), ysem, 0, other_y)
    for k in (1, 3, 2):
        for h in range(2):
            for w in range(2):
                y_ = y if w == 0 else 1 - y
                send(r_ref.at[0, pl.ds(32 * h, 32)], block(me, y, c, 32 * h, 32), u1, h * 6 + (k - 1) * 2 + w, at(place(h, k), y_, c))
    send(own, block(me, y, c, 0, 64), sib, 0, other_c)
    first = pltpu.make_async_remote_copy(src_ref=q_ref.at[pl.ds(0, TAIL)], dst_ref=qx.at[pl.ds(rows, TAIL)], send_sem=qsem.at[0],
                                         recv_sem=qsem.at[1], device_id={"pb": jnp.maximum(pb - 1, 0)}, device_id_type=MESH)

    @pl.when(pb > 0)
    def _():
        first.start()

    mine = pltpu.make_async_copy(q_ref, qx.at[pl.ds(0, rows)], local.at[1])
    mine.start()

    none = jnp.zeros((TAIL, E), BF)

    @pl.when(last)
    def _():
        qx[pl.ds(rows, TAIL), :] = none

    @pl.when(row == 1)
    def _():
        gv[32, pl.ds(0, TAIL), :] = none

    zero = jnp.zeros((PAD, 128), F32)

    def clear(b, _):
        s[b, pl.ds(all_rows, PAD), :] = zero
        return 0
    lax.fori_loop(0, PLANES, clear, 0)
    for b in range(PLANES, ZERO + 1):
        s[b] = jnp.zeros((all_rows + PAD, 128), F32)
    for d in range(NDIR):
        for k in range(4):
            ds[d][k] = jnp.zeros((all_rows + PAD, 128), F32)

    ri = iota((256, 256), 0)
    ci = iota((256, 256), 1)
    turn = jnp.where(((ri >> 3) == (ci & 31)) & ((ri & 7) == (ci >> 5)), 1.0, 0.0).astype(BF)

    def rearrange(chunk, shifted):
        k0 = 4 * chunk
        got = []
        for u in range(2):
            k = k0 + 2 * u
            if shifted:
                v = jnp.concatenate([gv[k, pl.ds(32, 96), :], gv[k + 1], gv[k + 2, pl.ds(0, 32), :]], axis=0)
            else:
                v = gv[pl.ds(k, 2)].reshape(256, E)
            planes = HALO if shifted else B
            got.append(jnp.dot(turn[:planes * 8], v, preferred_element_type=F32).reshape(planes, 8, E))
        lanes = pl.ds(pl.multiple_of(chunk * 16, 16), 16)
        rb[pl.ds(B if shifted else 0, got[0].shape[0]), lanes, :] = jnp.concatenate(got, axis=1).astype(BF)

    def slab(z_):
        def body(t, _):
            rearrange(2 * z_ + t, False)
            return 0
        lax.fori_loop(0, 2, body, 0)
        rearrange(2 * z_, True)

    steps = (0, 3, 1, 2)

    def onward(h, j, w, src, dst):
        send(src, dst, v1, w * 16 + h * 8 + 2 * j, at(spot(h, 0, 1), y, c))
        send(src, dst, v1, w * 16 + h * 8 + 2 * j + 1, at(spot(h, 0, 3), y, c))
        if w:
            send(src, dst, far, h * 4 + j, at(spot(h, 0, 2), y, c))

    for h in range(2):
        onward(h, 0, 0, r_ref.at[0, pl.ds(32 * h, 32)], block(me, y, c, 32 * h, 32))
    for j, k1 in enumerate(steps):
        for h in range(2):
            if k1:
                p = block(place(h, k1), y, c, 32 * h, 32)
                arrived(p, u1, h * 6 + (3 - k1) * 2)
                onward(h, j, 0, p, p)
    n = 2
    for j, k1 in enumerate(steps):
        if not k1:
            arrived(block(me, 1 - y, c, 0, 64), ysem, 0)
        for h in range(2):
            p = block(place(h, k1), 1 - y, c, 32 * h, 32)
            if k1:
                arrived(p, u1, h * 6 + (3 - k1) * 2 + 1)
            onward(h, j, 1, p, p)
            if k1:
                both = pair(place(h, k1), c, 32 * h, 32)
                send(both, both, sib, n, other_c)
                n += 1
    theirs = block(me, 1 - y, c, 0, 64)
    send(theirs, theirs, sib, 1, other_c)

    keep.wait()
    head = [pltpu.make_async_remote_copy(src_ref=gv.at[0, pl.ds(0, TAIL)], dst_ref=gv.at[32, pl.ds(0, TAIL)], send_sem=hsem.at[k],
                                         recv_sem=hsem.at[8], device_id={"pb": at((k >> 1, x), y, k & 1), "row": 0}, device_id_type=MESH)
            for k in range(8)]

    @pl.when((row == 1) & (z == 0) & (c == 0))
    def _():
        for copy in head:
            copy.start()

    for j, k1 in enumerate(steps):
        for h in range(2):
            for side, k2 in ((0, 3), (1, 1)):
                src = spot(h, k1, k2)
                arrived(block(src, y, c, 32 * h, 32), v1, h * 8 + 2 * j + side)
                piece = block(src, y, c, 32 * h + 16 * side, 16)
                send(piece, piece, v2, h * 8 + 2 * j + side, at(spot(h, 0, 1 if side == 0 else 3), y, c))
    for j, k1 in enumerate(steps):
        for h in range(2):
            for side, k2 in ((0, 3), (1, 1)):
                src = spot(h, k1, k2)
                arrived(block(src, 1 - y, c, 32 * h, 32), v1, 16 + h * 8 + 2 * j + side)
                both = pair(src, c, 32 * h, 32)
                send(both, both, sib, n, other_c)
                n += 1
    for j, k1 in enumerate(steps):
        for h in range(2):
            src = spot(h, k1, 2)
            for side in range(2):
                arrived(block(src, y, c, 32 * h + 16 * side, 16), v2, h * 8 + 2 * j + side)
            arrived(block(src, 1 - y, c, 32 * h, 32), far, h * 4 + j)
            both = pair(src, c, 32 * h, 32)
            send(both, both, sib, n, other_c)
            n += 1
    oc = 1 - c
    arrived(block(me, y, oc, 0, 64), sib, 0)
    arrived(block(me, 1 - y, oc, 0, 64), sib, 1)
    n = 2
    for k1 in steps[1:]:
        for h in range(2):
            arrived(pair(spot(h, k1, 0), oc, 32 * h, 32), sib, n)
            n += 1
    for k1 in steps:
        for h in range(2):
            for k2 in (3, 1):
                arrived(pair(spot(h, k1, k2), oc, 32 * h, 32), sib, n)
                n += 1
    for k1 in steps:
        for h in range(2):
            arrived(pair(spot(h, k1, 2), oc, 32 * h, 32), sib, n)
            n += 1
    for k in range(4):
        slab(k)

    @pl.when(row == 0)
    def _():
        head[0].wait_recv()

    @pl.when(pb < 63)
    def _():
        first.wait_recv()
    mine.wait()

    def edges(t, _):
        rearrange(2 * t + 1, True)
        return 0
    lax.fori_loop(0, 4, edges, 0)

    def dots(t, _):
        w = rb[pl.ds(GROUP * t, GROUP)].reshape(GROUP * 128, E)
        v = lax.dot_general(qx[...], w, (((1,), (1,)), ((), ())), preferred_element_type=F32)
        for u in range(GROUP):
            s[GROUP * t + u, pl.ds(0, all_rows), :] = v[:, u * 128:(u + 1) * 128]
        return 0
    lax.fori_loop(0, PLANES // GROUP, dots, 0)

    ps = [steps_ref[0, d] for d in range(NDIR)]
    ss = [steps_ref[1, d] for d in range(NDIR)]
    three = [jnp.maximum(ps[d], ss[d]) == 3 for d in range(NDIR)]
    ns = [jnp.where(three[d], lengths[d] // 3, lengths[d] // 2) for d in range(NDIR)]
    phase = [lengths[d] - ns[d] * jnp.where(three[d], 3, 2) for d in range(NDIR)]
    weight = [1.0 / (lengths[d].astype(F32)) * (1.0 / math.sqrt(E)) for d in range(NDIR)]

    def tap(v, other, times):
        return jnp.where(v > other, times, jnp.where(times * v >= other, 1, 0))
    q1 = [tap(ps[d], ss[d], 1) for d in range(NDIR)]
    r1 = [tap(ss[d], ps[d], 1) for d in range(NDIR)]
    q2 = [tap(ps[d], ss[d], 2) for d in range(NDIR)]
    r2 = [tap(ss[d], ps[d], 2) for d in range(NDIR)]

    def step(d, b, r, s0):
        dp = ds[d][(b + ss[d]) & 3, pl.ds(r + ps[d], SUPER), :]
        t2 = s[jnp.where(three[d], b + r2[d], ZERO), pl.ds(r + q2[d], SUPER), :]
        t1 = s[b + r1[d], pl.ds(r + q1[d], SUPER), :]
        x2 = dp + t2
        x1 = x2 + t1
        x0 = x1 + s0
        e = jnp.where(phase[d] == 0, x0, jnp.where(phase[d] == 1, x1, x2))
        ds[d][b & 3, pl.ds(r, SUPER), :] = x0
        es[d][b & 31, pl.ds(r, SUPER), :] = e
        return x0

    def past(k, _):
        b = PLANES - 1 - k
        for r in range(0, all_rows, SUPER):
            s0 = s[b, pl.ds(r, SUPER), :]
            for d in range(NDIR):
                step(d, b, r, s0)
        return 0
    lax.fori_loop(0, HALO, past, 0)

    def inside(k, _):
        b = B - 1 - k
        for r in range(0, all_rows, SUPER):
            s0 = s[b, pl.ds(r, SUPER), :]
            best = None
            for d in range(NDIR):
                x0 = step(d, b, r, s0)
                if r < rows:
                    en = es[d][(b + ns[d] * ss[d]) & 31, pl.ds(r + ns[d] * ps[d], SUPER), :]
                    v = (x0 - en) * weight[d]
                    best = v if best is None else jnp.maximum(best, v)
            if r < rows:
                o[b, pl.ds(r, SUPER), :] = best.astype(BF)
        return 0
    outs = []
    for k in range(4):
        lax.fori_loop(8 * k, 8 * k + 8, inside, 0)
        part = pl.ds(B - 8 * k - 8, 8)
        copy = pltpu.make_async_copy(o.at[part], o_ref.at[part], osem.at[k])
        copy.start()
        outs.append(copy)
    for copy in sends:
        copy.wait_send()

    @pl.when(pb > 0)
    def _():
        first.wait_send()

    @pl.when((row == 1) & (z == 0) & (c == 0))
    def _():
        for copy in head:
            copy.wait_send()
    for copy in outs:
        copy.wait()


def untangle(o_ref, out_ref, o, perm, flat, isem, osem):
    rows = o_ref.shape[1]
    parts = 2
    size = rows // parts
    ins = [pltpu.make_async_copy(o_ref.at[:, pl.ds(k * size, size)], o.at[:, pl.ds(k * size, size)], isem.at[k]) for k in range(parts)]
    for copy in ins:
        copy.start()
    la = iota((128, 128), 0)
    ll = iota((128, 128), 1)
    same = (la & 3) == (ll >> 5)

    def make(q, _):
        perm[q] = jnp.where(same & (((la >> 2) ^ (ll & 31)) == q), 1.0, 0.0).astype(BF)
        return 0
    lax.fori_loop(0, B, make, 0)
    lane = iota((16, 128), 1)
    bit = [((lane >> t) & 1).astype(F32).astype(BF) for t in range(7)]

    def network(v, bits):
        for t in range(5):
            mask = bit[bits + t] > 0.5
            v = [jnp.where(mask, v[q ^ (1 << t)], v[q]) for q in range(B)]
        return v
    outs = []
    for k in range(parts):
        ins[k].wait()

        def skew(i, _):
            r = pl.ds(pl.multiple_of(k * size + i * 16, 16), 16)
            v = network([o[q, r, :] for q in range(B)], 2)
            for q in range(B):
                o[q, r, :] = v[q]
            return 0
        lax.fori_loop(0, size // 16, skew, 0)

        def lanes(t, _):
            r = pl.ds(k * size, size)
            got = [jnp.dot(o[8 * t + u, r, :], perm[8 * t + u], preferred_element_type=F32).astype(BF) for u in range(8)]
            for u in range(8):
                o[8 * t + u, r, :] = got[u]
            return 0
        lax.fori_loop(0, B // 8, lanes, 0)

        def back(i, _):
            r = pl.ds(pl.multiple_of(k * size + i * 16, 16), 16)
            v = network([o[q, r, :] for q in range(B)], 0)
            for q in range(B):
                flat[r, q * 128:(q + 1) * 128] = v[q]
            return 0
        lax.fori_loop(0, size // 16, back, 0)
        part = pl.ds(k * size, size)
        copy = pltpu.make_async_copy(flat.at[part], out_ref.at[part], osem.at[k])
        copy.start()
        outs.append(copy)
    for copy in outs:
        copy.wait()


def per_device(queries, references, ratios, lengths):
    rows = queries.shape[0]
    cols = references.shape[1] * 64
    V, D, ANY = pltpu.VMEM, pltpu.SemaphoreType.DMA, pl.BlockSpec(memory_space=pl.ANY)
    all_rows = rows + TAIL
    o = pl.pallas_call(
        gather_and_smooth,
        out_shape=jax.ShapeDtypeStruct((B, rows, 128), BF),
        in_specs=[pl.BlockSpec(memory_space=pltpu.SMEM)] * 2 + [ANY] * 2,
        out_specs=ANY,
        scratch_shapes=[V((33, 128, E), BF), V((all_rows, E), BF), V((PLANES, 128, E), BF), V((ZERO + 1, all_rows + PAD, 128), F32)]
        + [V((4, all_rows + PAD, 128), F32)] * 4 + [V((32, all_rows + PAD, 128), F32)] * 4 + [V((B, rows, 128), BF)]
        + [D((2,)), D((2, 1)), D((2, 12)), D((2, 32)), D((2, 8)), D((2, 16)), D((2, 32)), D((2,)), D((9,)), D((4,))],
        compiler_params=pltpu.CompilerParams(collective_id=0, has_side_effects=True, vmem_limit_bytes=60 * 1024 * 1024),
        name="gather_and_smooth",
    )(ratios.T, lengths, queries, references)
    return pl.pallas_call(
        untangle,
        out_shape=jax.ShapeDtypeStruct((rows, cols), BF),
        in_specs=[ANY],
        out_specs=ANY,
        scratch_shapes=[V((B, rows, 128), BF), V((B, 128, 128), BF), V((rows, cols), BF), D((2,)), D((2,))],
        compiler_params=pltpu.CompilerParams(vmem_limit_bytes=60 * 1024 * 1024),
        name="untangle",
    )(o)


def solution(mesh):
    placed = (P("pb", None), P("row", "pb", None), P(), P())
    return jax.shard_map(
        per_device, mesh=mesh, in_specs=placed, out_specs=P("pb", "row"), check_vma=False
    )
```

time: 823 us -> 51.7 us (0.06); the launches traced: 813 us -> 51.6 us
  other arithmetic: 415 us -> 0 us
  between operations: 374 us -> 0.01 us
  Pallas kernels: 0 us -> 51.6 us
  local copies, waits for them, and re-layouts: 14.3 us -> 0 us
    convert_element_type x1 -> x0, other arithmetic: 409 us -> none  [one_block(): return smooth(similarity, along_query, along_ref, tap_weights, block_rows...]
    pallas_call x0 -> x2, Pallas kernels: none -> 51.6 us  [the longest x1 46.1 us: per_device(): pl.pallas_call(gather_and_smooth, out_shape=jax.ShapeDtypeStruct((B, rows...]
    slice x20 -> x0, local copies, waits for them, and re-layouts: 14.3 us -> none  [the longest x6 4.35 us: smooth(): along_ref[direction, tap_index]]
  transfers between devices with their start and end apart: 3 -> 0, of which waited for: 0 -> 0; matrix products, arithmetic and copies ran while one was open for 2% -> 0% of each run, Pallas kernels for 0% -> 0%
where the time goes in v2:
time: 51.7 us; the launch traced here: 51.6 us
  Pallas kernels  51.6 us (100%)
    pallas_call x1, Pallas kernels, per_device(): pl.pallas_call(gather_and_smooth, out_shape=jax.ShapeDtypeStruct((B, rows...  46.1 us
    pallas_call x1, Pallas kernels, per_device(): pl.pallas_call(untangle, out_shape=jax.ShapeDtypeStruct((rows, cols), BF)...  5.5 us

profile of v2, /device:TPU:1, one launch (start us, length us, event | category | flops | bytes accessed | tf_op | source)
XLA Modules:
  0.0 51.6 jit_solution(16277934042316893048)
XLA Ops:
  0.0 46.1 %gather_and_smooth.1.o_ref = bf16[32,256,128]{2,1,0:T(8,128)(2,1)} custom-call(s32[2,4]{1,0:T(2,128)} %bitcast.1, s32[4]{0:T(128)} %lengths.1, bf16[256,512]{1,0:T(8,128)(2,1)} %q_ref.1, bf16[1,64,512]{2,1,0:T(8,128)(2,1)} %r_ref.1), custom_call_target="tpu_custom_call" | custom-call | tf_op jit(solution)/shard_map/gather_and_smooth/pallas_call | solution.py:392
  46.1 5.5 %untangle.1 = bf16[256,4096]{1,0:T(8,128)(2,1)} custom-call(bf16[32,256,128]{2,1,0:T(8,128)(2,1)} %gather_and_smooth.1.o_ref), custom_call_target="tpu_custom_call" | custom-call | tf_op jit(solution)/shard_map/untangle/pallas_call | solution.py:403

commit v3 on v2

--- a/solution.py
+++ b/solution.py
@@ -16,7 +16,7 @@
 TAIL = 32
 PAD = 8
 SUPER = 32
-GROUP = 8
+GROUP = 28
 MESH = pl.DeviceIdType.MESH
 F32, BF = jnp.float32, jnp.bfloat16
 
@@ -126,26 +126,27 @@
     ci = iota((256, 256), 1)
     turn = jnp.where(((ri >> 3) == (ci & 31)) & ((ri & 7) == (ci >> 5)), 1.0, 0.0).astype(BF)
 
-    def rearrange(chunk, shifted):
-        k0 = 4 * chunk
+    def rearrange(h, group, shifted):
         got = []
         for u in range(2):
-            k = k0 + 2 * u
-            if shifted:
-                v = jnp.concatenate([gv[k, pl.ds(32, 96), :], gv[k + 1], gv[k + 2, pl.ds(0, 32), :]], axis=0)
-            else:
-                v = gv[pl.ds(k, 2)].reshape(256, E)
+            rows_of = []
+            for i in range(4):
+                hi, y_ = 2 * u + (i >> 1), i & 1
+                k = (8 * group + 2 * hi if h == 0 else 8 * hi + 2 * group) + y_
+                for core in range(2):
+                    if not shifted:
+                        part = gv[k, pl.ds(64 * core + 32 * h, 32), :]
+                    elif h == 0:
+                        part = gv[k, pl.ds(64 * core + 32, 32), :]
+                    elif core == 0:
+                        part = gv[k, pl.ds(64, 32), :]
+                    else:
+                        part = gv[k + 1, pl.ds(0, 32), :]
+                    rows_of.append(part)
             planes = HALO if shifted else B
-            got.append(jnp.dot(turn[:planes * 8], v, preferred_element_type=F32).reshape(planes, 8, E))
-        lanes = pl.ds(pl.multiple_of(chunk * 16, 16), 16)
+            got.append(jnp.dot(turn[:planes * 8], jnp.concatenate(rows_of, axis=0), preferred_element_type=F32).reshape(planes, 8, E))
+        lanes = pl.ds(pl.multiple_of(64 * h + group * 16, 16), 16)
         rb[pl.ds(B if shifted else 0, got[0].shape[0]), lanes, :] = jnp.concatenate(got, axis=1).astype(BF)
-
-    def slab(z_):
-        def body(t, _):
-            rearrange(2 * z_ + t, False)
-            return 0
-        lax.fori_loop(0, 2, body, 0)
-        rearrange(2 * z_, True)
 
     steps = (0, 3, 1, 2)
 
@@ -204,6 +205,24 @@
                 both = pair(src, c, 32 * h, 32)
                 send(both, both, sib, n, other_c)
                 n += 1
+    oc = 1 - c
+    arrived(block(me, y, oc, 0, 64), sib, 0)
+    arrived(block(me, 1 - y, oc, 0, 64), sib, 1)
+    n2 = 2
+    for k1 in steps[1:]:
+        for h in range(2):
+            arrived(pair(place(h, k1), oc, 32 * h, 32), sib, n2)
+            n2 += 1
+    rearrange(0, z, False)
+    rearrange(1, x, False)
+    for k1 in steps:
+        for h in range(2):
+            for k2 in (3, 1):
+                arrived(pair(spot(h, k1, k2), oc, 32 * h, 32), sib, n2)
+                n2 += 1
+    for k in (3, 1):
+        rearrange(0, (z + k) & 3, False)
+        rearrange(1, (x + k) & 3, False)
     for j, k1 in enumerate(steps):
         for h in range(2):
             src = spot(h, k1, 2)
@@ -213,25 +232,12 @@
             both = pair(src, c, 32 * h, 32)
             send(both, both, sib, n, other_c)
             n += 1
-    oc = 1 - c
-    arrived(block(me, y, oc, 0, 64), sib, 0)
-    arrived(block(me, 1 - y, oc, 0, 64), sib, 1)
-    n = 2
-    for k1 in steps[1:]:
-        for h in range(2):
-            arrived(pair(spot(h, k1, 0), oc, 32 * h, 32), sib, n)
-            n += 1
     for k1 in steps:
         for h in range(2):
-            for k2 in (3, 1):
-                arrived(pair(spot(h, k1, k2), oc, 32 * h, 32), sib, n)
-                n += 1
-    for k1 in steps:
-        for h in range(2):
-            arrived(pair(spot(h, k1, 2), oc, 32 * h, 32), sib, n)
-            n += 1
-    for k in range(4):
-        slab(k)
+            arrived(pair(spot(h, k1, 2), oc, 32 * h, 32), sib, n2)
+            n2 += 1
+    rearrange(0, (z + 2) & 3, False)
+    rearrange(1, (x + 2) & 3, False)
 
     @pl.when(row == 0)
     def _():
@@ -243,7 +249,8 @@
     mine.wait()
 
     def edges(t, _):
-        rearrange(2 * t + 1, True)
+        for h in range(2):
+            rearrange(h, t, True)
         return 0
     lax.fori_loop(0, 4, edges, 0)
 
@@ -282,16 +289,20 @@
         return x0
 
     def past(k, _):
-        b = PLANES - 1 - k
-        for r in range(0, all_rows, SUPER):
-            s0 = s[b, pl.ds(r, SUPER), :]
-            for d in range(NDIR):
-                step(d, b, r, s0)
-        return 0
-    lax.fori_loop(0, HALO, past, 0)
+        for b in (PLANES - 1 - 2 * k, PLANES - 2 - 2 * k):
+            for r in range(0, all_rows, SUPER):
+                s0 = s[b, pl.ds(r, SUPER), :]
+                for d in range(NDIR):
+                    step(d, b, r, s0)
+        return 0
+    lax.fori_loop(0, HALO // 2, past, 0)
 
     def inside(k, _):
-        b = B - 1 - k
+        for b in (B - 1 - 2 * k, B - 2 - 2 * k):
+            within(b)
+        return 0
+
+    def within(b):
         for r in range(0, all_rows, SUPER):
             s0 = s[b, pl.ds(r, SUPER), :]
             best = None
@@ -303,10 +314,9 @@
                     best = v if best is None else jnp.maximum(best, v)
             if r < rows:
                 o[b, pl.ds(r, SUPER), :] = best.astype(BF)
-        return 0
     outs = []
     for k in range(4):
-        lax.fori_loop(8 * k, 8 * k + 8, inside, 0)
+        lax.fori_loop(4 * k, 4 * k + 4, inside, 0)
         part = pl.ds(B - 8 * k - 8, 8)
         copy = pltpu.make_async_copy(o.at[part], o_ref.at[part], osem.at[k])
         copy.start()
@@ -335,18 +345,22 @@
         copy.start()
     la = iota((128, 128), 0)
     ll = iota((128, 128), 1)
-    same = (la & 3) == (ll >> 5)
+
+    def block_of(lane):
+        n = lane & 63
+        return jnp.where(lane < 64, n, ((n >> 2) & 3) * 16 + (n >> 4) * 4 + (n & 3))
+    same = (block_of(la) & 1) * 2 + (la >> 6) == (ll >> 5)
 
     def make(q, _):
-        perm[q] = jnp.where(same & (((la >> 2) ^ (ll & 31)) == q), 1.0, 0.0).astype(BF)
+        perm[q] = jnp.where(same & (((block_of(la) >> 1) ^ (ll & 31)) == q), 1.0, 0.0).astype(BF)
         return 0
     lax.fori_loop(0, B, make, 0)
     lane = iota((16, 128), 1)
-    bit = [((lane >> t) & 1).astype(F32).astype(BF) for t in range(7)]
-
-    def network(v, bits):
+    bit = [[((v >> t) & 1).astype(F32).astype(BF) for t in range(5)] for v in (block_of(lane) >> 1, lane)]
+
+    def network(v, way):
         for t in range(5):
-            mask = bit[bits + t] > 0.5
+            mask = bit[way][t] > 0.5
             v = [jnp.where(mask, v[q ^ (1 << t)], v[q]) for q in range(B)]
         return v
     outs = []
@@ -355,7 +369,7 @@
 
         def skew(i, _):
             r = pl.ds(pl.multiple_of(k * size + i * 16, 16), 16)
-            v = network([o[q, r, :] for q in range(B)], 2)
+            v = network([o[q, r, :] for q in range(B)], 0)
             for q in range(B):
                 o[q, r, :] = v[q]
             return 0
@@ -363,15 +377,15 @@
 
         def lanes(t, _):
             r = pl.ds(k * size, size)
-            got = [jnp.dot(o[8 * t + u, r, :], perm[8 * t + u], preferred_element_type=F32).astype(BF) for u in range(8)]
-            for u in range(8):
-                o[8 * t + u, r, :] = got[u]
+            got = [jnp.dot(o[32 * t + u, r, :], perm[32 * t + u], preferred_element_type=F32).astype(BF) for u in range(32)]
+            for u in range(32):
+                o[32 * t + u, r, :] = got[u]
             return 0
-        lax.fori_loop(0, B // 8, lanes, 0)
+        lax.fori_loop(0, B // 32, lanes, 0)
 
         def back(i, _):
             r = pl.ds(pl.multiple_of(k * size + i * 16, 16), 16)
-            v = network([o[q, r, :] for q in range(B)], 0)
+            v = network([o[q, r, :] for q in range(B)], 1)
             for q in range(B):
                 flat[r, q * 128:(q + 1) * 128] = v[q]
             return 0

time: 51.7 us -> 47.6 us (0.921)
  Pallas kernels: 51.6 us -> 47.4 us
    pallas_call x1, Pallas kernels: 46.1 us -> 42.8 us  [per_device(): pl.pallas_call(gather_and_smooth, out_shape=jax.ShapeDtypeStruct((B, rows...]
    pallas_call x1, Pallas kernels: 5.5 us -> 4.6 us  [per_device(): pl.pallas_call(untangle, out_shape=jax.ShapeDtypeStruct((rows, cols), BF)...]
where the time goes in v3:
time: 47.6 us; the launch traced here: 47.4 us
  Pallas kernels  47.4 us (100%)
    pallas_call x1, Pallas kernels, per_device(): pl.pallas_call(gather_and_smooth, out_shape=jax.ShapeDtypeStruct((B, rows...  42.8 us
    pallas_call x1, Pallas kernels, per_device(): pl.pallas_call(untangle, out_shape=jax.ShapeDtypeStruct((rows, cols), BF)...  4.6 us

profile of v3, /device:TPU:1, one launch (start us, length us, event | category | flops | bytes accessed | tf_op | source)
XLA Modules:
  0.0 47.4 jit_solution(12836735234210116767)
XLA Ops:
  0.0 42.8 %gather_and_smooth.1.o_ref = bf16[32,256,128]{2,1,0:T(8,128)(2,1)} custom-call(s32[2,4]{1,0:T(2,128)} %bitcast.1, s32[4]{0:T(128)} %lengths.1, bf16[256,512]{1,0:T(8,128)(2,1)} %q_ref.1, bf16[1,64,512]{2,1,0:T(8,128)(2,1)} %r_ref.1), custom_call_target="tpu_custom_call" | custom-call | tf_op jit(solution)/shard_map/gather_and_smooth/pallas_call | solution.py:406
  42.8 4.6 %untangle.1 = bf16[256,4096]{1,0:T(8,128)(2,1)} custom-call(bf16[32,256,128]{2,1,0:T(8,128)(2,1)} %gather_and_smooth.1.o_ref), custom_call_target="tpu_custom_call" | custom-call | tf_op jit(solution)/shard_map/untangle/pallas_call | solution.py:417

commit v4 on v3

--- a/solution.py
+++ b/solution.py
@@ -16,7 +16,7 @@
 TAIL = 32
 PAD = 8
 SUPER = 32
-GROUP = 28
+GROUP = 56
 MESH = pl.DeviceIdType.MESH
 F32, BF = jnp.float32, jnp.bfloat16
 
@@ -236,31 +236,30 @@
         for h in range(2):
             arrived(pair(spot(h, k1, 2), oc, 32 * h, 32), sib, n2)
             n2 += 1
+
+    @pl.when(row == 0)
+    def _():
+        head[0].wait_recv()
+
+    @pl.when(pb < 63)
+    def _():
+        first.wait_recv()
+    mine.wait()
+
     rearrange(0, (z + 2) & 3, False)
     rearrange(1, (x + 2) & 3, False)
 
-    @pl.when(row == 0)
-    def _():
-        head[0].wait_recv()
-
-    @pl.when(pb < 63)
-    def _():
-        first.wait_recv()
-    mine.wait()
-
-    def edges(t, _):
+    for t in range(4):
         for h in range(2):
             rearrange(h, t, True)
-        return 0
-    lax.fori_loop(0, 4, edges, 0)
-
-    def dots(t, _):
+
+    def dots(t):
         w = rb[pl.ds(GROUP * t, GROUP)].reshape(GROUP * 128, E)
         v = lax.dot_general(qx[...], w, (((1,), (1,)), ((), ())), preferred_element_type=F32)
         for u in range(GROUP):
             s[GROUP * t + u, pl.ds(0, all_rows), :] = v[:, u * 128:(u + 1) * 128]
-        return 0
-    lax.fori_loop(0, PLANES // GROUP, dots, 0)
+    for t in range(PLANES // GROUP):
+        dots(t)
 
     ps = [steps_ref[0, d] for d in range(NDIR)]
     ss = [steps_ref[1, d] for d in range(NDIR)]

time: 47.6 us -> 46.4 us (0.975)
  Pallas kernels: 47.4 us -> 46.3 us
    pallas_call x1, Pallas kernels: 42.8 us -> 41.7 us  [per_device(): pl.pallas_call(gather_and_smooth, out_shape=jax.ShapeDtypeStruct((B, rows...]
where the time goes in v4:
time: 46.4 us; the launch traced here: 46.3 us
  Pallas kernels  46.3 us (100%)
    pallas_call x1, Pallas kernels, per_device(): pl.pallas_call(gather_and_smooth, out_shape=jax.ShapeDtypeStruct((B, rows...  41.7 us
    pallas_call x1, Pallas kernels, per_device(): pl.pallas_call(untangle, out_shape=jax.ShapeDtypeStruct((rows, cols), BF)...  4.6 us

profile of v4, /device:TPU:1, one launch (start us, length us, event | category | flops | bytes accessed | tf_op | source)
XLA Modules:
  0.0 46.3 jit_solution(539709909590952491)
XLA Ops:
  0.0 41.7 %gather_and_smooth.1.o_ref = bf16[32,256,128]{2,1,0:T(8,128)(2,1)} custom-call(s32[2,4]{1,0:T(2,128)} %bitcast.1, s32[4]{0:T(128)} %lengths.1, bf16[256,512]{1,0:T(8,128)(2,1)} %q_ref.1, bf16[1,64,512]{2,1,0:T(8,128)(2,1)} %r_ref.1), custom_call_target="tpu_custom_call" | custom-call | tf_op jit(solution)/shard_map/gather_and_smooth/pallas_call | solution.py:405
  41.7 4.6 %untangle.1 = bf16[256,4096]{1,0:T(8,128)(2,1)} custom-call(bf16[32,256,128]{2,1,0:T(8,128)(2,1)} %gather_and_smooth.1.o_ref), custom_call_target="tpu_custom_call" | custom-call | tf_op jit(solution)/shard_map/untangle/pallas_call | solution.py:416

commit v5 on v4

--- a/solution.py
+++ b/solution.py
@@ -220,9 +220,6 @@
             for k2 in (3, 1):
                 arrived(pair(spot(h, k1, k2), oc, 32 * h, 32), sib, n2)
                 n2 += 1
-    for k in (3, 1):
-        rearrange(0, (z + k) & 3, False)
-        rearrange(1, (x + k) & 3, False)
     for j, k1 in enumerate(steps):
         for h in range(2):
             src = spot(h, k1, 2)
@@ -232,6 +229,9 @@
             both = pair(src, c, 32 * h, 32)
             send(both, both, sib, n, other_c)
             n += 1
+    for k in (3, 1):
+        rearrange(0, (z + k) & 3, False)
+        rearrange(1, (x + k) & 3, False)
     for k1 in steps:
         for h in range(2):
             arrived(pair(spot(h, k1, 2), oc, 32 * h, 32), sib, n2)
@@ -288,16 +288,16 @@
         return x0
 
     def past(k, _):
-        for b in (PLANES - 1 - 2 * k, PLANES - 2 - 2 * k):
+        for b in [PLANES - 1 - u - 4 * k for u in range(4)]:
             for r in range(0, all_rows, SUPER):
                 s0 = s[b, pl.ds(r, SUPER), :]
                 for d in range(NDIR):
                     step(d, b, r, s0)
         return 0
-    lax.fori_loop(0, HALO // 2, past, 0)
+    lax.fori_loop(0, HALO // 4, past, 0)
 
     def inside(k, _):
-        for b in (B - 1 - 2 * k, B - 2 - 2 * k):
+        for b in [B - 1 - u - 4 * k for u in range(4)]:
             within(b)
         return 0
 
@@ -315,7 +315,7 @@
                 o[b, pl.ds(r, SUPER), :] = best.astype(BF)
     outs = []
     for k in range(4):
-        lax.fori_loop(4 * k, 4 * k + 4, inside, 0)
+        lax.fori_loop(2 * k, 2 * k + 2, inside, 0)
         part = pl.ds(B - 8 * k - 8, 8)
         copy = pltpu.make_async_copy(o.at[part], o_ref.at[part], osem.at[k])
         copy.start()

time: 46.4 us -> 45.5 us (0.981)
  Pallas kernels: 46.3 us -> 45.4 us
    pallas_call x1, Pallas kernels: 41.7 us -> 40.8 us  [per_device(): pl.pallas_call(gather_and_smooth, out_shape=jax.ShapeDtypeStruct((B, rows...]
where the time goes in v5:
time: 45.5 us; the launch traced here: 45.4 us
  Pallas kernels  45.4 us (100%)
    pallas_call x1, Pallas kernels, per_device(): pl.pallas_call(gather_and_smooth, out_shape=jax.ShapeDtypeStruct((B, rows...  40.8 us
    pallas_call x1, Pallas kernels, per_device(): pl.pallas_call(untangle, out_shape=jax.ShapeDtypeStruct((rows, cols), BF)...  4.6 us

profile of v5, /device:TPU:1, one launch (start us, length us, event | category | flops | bytes accessed | tf_op | source)
XLA Modules:
  0.0 45.4 jit_solution(8598743593911505211)
XLA Ops:
  0.0 40.8 %gather_and_smooth.1.o_ref = bf16[32,256,128]{2,1,0:T(8,128)(2,1)} custom-call(s32[2,4]{1,0:T(2,128)} %bitcast.1, s32[4]{0:T(128)} %lengths.1, bf16[256,512]{1,0:T(8,128)(2,1)} %q_ref.1, bf16[1,64,512]{2,1,0:T(8,128)(2,1)} %r_ref.1), custom_call_target="tpu_custom_call" | custom-call | tf_op jit(solution)/shard_map/gather_and_smooth/pallas_call | solution.py:405
  40.8 4.6 %untangle.1 = bf16[256,4096]{1,0:T(8,128)(2,1)} custom-call(bf16[32,256,128]{2,1,0:T(8,128)(2,1)} %gather_and_smooth.1.o_ref), custom_call_target="tpu_custom_call" | custom-call | tf_op jit(solution)/shard_map/untangle/pallas_call | solution.py:416
